TPU v7x, 256 devices: a whole 4x4x8 slice. The times are simulated.
256 devices in a mesh: dp: 4 (over y), gx: 4 (over x), gy: 16 (over z, core).
Axes of the slice: x: 4, y: 4, z: 8, core: 2. Of those that a mesh axis runs over, the one named last changes fastest.
Arguments:
- field: bfloat16 [4, 64, 32, 20, 2048], P('dp', 'gx', 'gy'), may hold values from -6 to 6
- cotangent: bfloat16 [4, 64, 32, 20, 2048], P('dp', 'gx', 'gy'), may hold values from -6 to 6
- spectral_weight: bfloat16 [24, 24, 20, 20, 192], P(None, None, None, None, ('gx', 'gy')), may hold values from -2.5 to 2.5
- bypass_weight: bfloat16 [20, 20], replicated, may hold values from -1.25 to 1.25
Outputs:
- grad_field: bfloat16 [4, 64, 32, 20, 2048], P('dp', 'gx', 'gy')
- grad_spectral: float32 [24, 24, 20, 20, 192], P(None, None, None, None, ('gx', 'gy'))
- grad_bypass: float32 [20, 20], replicated
All inputs are finite; a program needn't handle non-finite values.
Results may differ from a plain program's by a relative error of at most 0.034.
Values may be sent and summed in bfloat16 or wider, within the bound.
No kernel may reach another device: no remote copies, remote signals or barrier semaphores. Data moves between devices by JAX's collectives and lax.ppermute only.
A program may use at most 192 MiB of HBM per device.

v0:
```python
import math
import jax
import jax.numpy as jnp
from jax import lax
from jax.sharding import PartitionSpec as P

MX = 12
MY = 12
MZ = 12
MT = 4
NZ = 128
NT = 16


def basis(length, kept):
    places = lax.iota(jnp.int32, length)
    orders = lax.iota(jnp.int32, kept)
    cos_arg = places[:, None] * orders[None, :] % length
    sin_arg = places[:, None] * (orders[None, :] + 1) % length
    step_angle = 2.0 * math.pi / length
    scale = math.sqrt(2.0 / length)
    cos_part = jnp.cos(cos_arg.astype(jnp.float32) * step_angle)
    sin_part = jnp.sin(sin_arg.astype(jnp.float32) * step_angle)
    return jnp.concatenate([cos_part, sin_part], axis=1) * scale


def mode_dot(form, data, table):
    upper = table.astype(jnp.bfloat16)
    lower = (table - upper.astype(jnp.float32)).astype(jnp.bfloat16)
    first = jnp.einsum(form, data, upper, preferred_element_type=jnp.float32)
    return first + jnp.einsum(form, data, lower, preferred_element_type=jnp.float32)


def body(field, cotangent, spectral_weight, bypass_weight):
    cells_x = field.shape[1]
    cells_y = field.shape[2]
    channels = field.shape[3]
    parts_x = lax.axis_size("gx")
    parts_y = lax.axis_size("gy")
    table_x = basis(cells_x * parts_x, MX)
    table_y = basis(cells_y * parts_y, MY)
    table_z = basis(NZ, MZ)
    table_t = basis(NT, MT)
    modes_zt = 4 * MZ * MT
    table_zt = (table_z[:, None, :, None] * table_t[None, :, None, :]).reshape(NZ * NT, modes_zt)

    def analyze(cells):
        matrix = cells.reshape(-1, NZ * NT)
        coeff = mode_dot("rp,pq->rq", matrix, table_zt).astype(jnp.bfloat16)
        coeff = coeff.reshape(cells_x, cells_y, channels, modes_zt)
        along_x = lax.all_to_all(coeff, "gx", split_axis=3, concat_axis=0, tiled=True)
        partial_x = mode_dot("xycq,xk->kycq", along_x, table_x).astype(jnp.bfloat16)
        along_y = lax.all_to_all(partial_x, "gy", split_axis=3, concat_axis=1, tiled=True)
        return mode_dot("kycq,yl->klcq", along_y, table_y).astype(jnp.bfloat16)

    def synthesize(spectrum):
        partial_y = mode_dot("klcq,yl->kycq", spectrum, table_y).astype(jnp.bfloat16)
        returned = lax.all_to_all(partial_y, "gy", split_axis=1, concat_axis=3, tiled=True)
        partial_x = mode_dot("kycq,xk->xycq", returned, table_x).astype(jnp.bfloat16)
        coeff = lax.all_to_all(partial_x, "gx", split_axis=0, concat_axis=3, tiled=True)
        matrix = coeff.reshape(-1, modes_zt)
        values = mode_dot("rq,pq->rp", matrix, table_zt)
        return values.reshape(1, cells_x, cells_y, channels, NZ * NT)

    spectrum = analyze(field)
    mixed = jnp.einsum(
        "klcq,klcoq->kloq", spectrum, spectral_weight, preferred_element_type=jnp.float32
    ).astype(jnp.bfloat16)
    spatial = synthesize(mixed)
    bypass = jnp.einsum("bxyip,io->bxyop", field, bypass_weight, preferred_element_type=jnp.float32)
    pre = spatial + bypass
    unused, pullback = jax.vjp(jax.nn.gelu, pre)
    (slope,) = pullback(cotangent.astype(jnp.float32))
    upstream = slope.astype(jnp.bfloat16)
    bypass_term = jnp.einsum("bxyip,bxyop->io", field, upstream, preferred_element_type=jnp.float32)
    grad_bypass = lax.psum(bypass_term, ("dp", "gx", "gy"))
    spectrum_up = analyze(upstream)
    local_grad = jnp.einsum(
        "klcq,kloq->klcoq", spectrum, spectrum_up, preferred_element_type=jnp.float32
    )
    grad_spectral = lax.psum(local_grad.astype(jnp.bfloat16), "dp").astype(jnp.float32)
    spectrum_back = jnp.einsum(
        "kloq,klcoq->klcq", spectrum_up, spectral_weight, preferred_element_type=jnp.float32
    ).astype(jnp.bfloat16)
    through_bypass = jnp.einsum(
        "bxyop,io->bxyip", upstream, bypass_weight, preferred_element_type=jnp.float32
    )
    grad_field = (synthesize(spectrum_back) + through_bypass).astype(jnp.bfloat16)
    return (grad_field, grad_spectral, grad_bypass)


def solution(mesh):
    in_specs = (
        P("dp", "gx", "gy", None, None),
        P("dp", "gx", "gy", None, None),
        P(None, None, None, None, ("gx", "gy")),
        P(),
    )
    out_specs = (P("dp", "gx", "gy", None, None), P(None, None, None, None, ("gx", "gy")), P())
    return jax.shard_map(body, mesh=mesh, in_specs=in_specs, out_specs=out_specs, check_vma=False)
```

profile of v0, /device:TPU:1, one launch (start us, length us, event | category | flops | bytes accessed | tf_op | source)
XLA Modules:
  0.0 493.5 jit_solution(16601009664940160456)
XLA Ops:
  7.5 4.7 copy.145
  15.8 6.2 %fusion = (bf16[128,16,24,8]{1,0,3,2:T(8,128)(2,1)}, bf16[128,16,24,8]{1,0,3,2:T(8,128)(2,1)}) fusion(f32[16,8]{0,1:T(8,128)S(1)} %maximum_multiply_fusion.3, f32[128,24]{0,1:T(8,128)S(1)} %maximum_multiply_fusion.2), kind=kLoop, calls=%fused_computation.5 | loop fusion | flops 1966080 | bytes 1585664 | tf_op jit(solution)/shard_map/convert_element_type | solution.py:29
  22.0 11.6 %convert_element_type.256 = bf16[2048,192]{0,1:T(8,128)(2,1)S(1)} reshape(bf16[128,16,24,8]{1,0,3,2:T(8,128)(2,1)} %get-tuple-element.26) | data formatting | bytes 1572864 | tf_op jit(solution)/shard_map/convert_element_type | solution.py:29
  33.7 12.3 %convert_element_type.253 = bf16[2048,192]{0,1:T(8,128)(2,1)} reshape(bf16[128,16,24,8]{1,0,3,2:T(8,128)(2,1)} %get-tuple-element.27) | data formatting | bytes 1572864 | tf_op jit(solution)/shard_map/convert_element_type | solution.py:28
  49.9 5.9 %reshape.160 = bf16[16,2,20,192]{2,1,0,3:T(2,128)(2,1)S(1)} reshape(bf16[640,192]{0,1:T(8,128)(2,1)} %fusion.30) | data formatting | bytes 491520 | tf_op jit(solution)/shard_map/reshape | solution.py:50
  55.9 4.2 reshape.162
  60.0 4.8 all-to-all-start
  65.0 5.3 %all-to-all-done = bf16[4,2,15360]{2,1,0:T(2,128)(2,1)S(1)} async-done(((bf16[4,2,15360]{2,1,0:T(2,128)(2,1)}), bf16[4,2,15360]{2,1,0:T(2,128)(2,1)S(1)}, u32[]{:S(2)}, u32[]{:S(2)}) %all-to-all-start) | async-done | bytes 245792 | tf_op jit(solution)/shard_map/all_to_all | solution.py:51
  70.3 4.1 reshape.163
  79.3 10.9 %all-to-all-start.1 = ((bf16[16,2,1440]{2,1,0:T(2,128)(2,1)}), bf16[16,2,1440]{2,1,0:T(2,128)(2,1)S(1)}, u32[]{:S(2)}, u32[]{:S(2)}) async-start(bf16[16,2,1440]{2,1,0:T(2,128)(2,1)} %reshape.164), calls=%async_computation.1 | async-start | bytes 196608 | tf_op jit(solution)/shard_map/all_to_all | solution.py:53
  90.4 8.2 %all-to-all-done.1 = bf16[16,2,1440]{2,1,0:T(2,128)(2,1)S(1)} async-done(((bf16[16,2,1440]{2,1,0:T(2,128)(2,1)}), bf16[16,2,1440]{2,1,0:T(2,128)(2,1)S(1)}, u32[]{:S(2)}, u32[]{:S(2)}) %all-to-all-start.1) | async-done | bytes 92192 | tf_op jit(solution)/shard_map/all_to_all | solution.py:53
  101.2 5.0 %multiply_reduce_fusion.1 = bf16[24,24,3,20]{1,0,2,3:T(8,128)(2,1)S(1)} fusion(f32[24,24,3,20]{1,0,2,3:T(8,128)S(1)} %copy.223, bf16[24,24,20,20,3]{1,0,4,3,2:T(8,128)(2,1)} %param.6), kind=kLoop, calls=%fused_computation.3 | loop fusion | flops 2039040 | bytes 1589760 | tf_op jit(solution)/shard_map/klcq,klcoq->kloq/dot_general | solution.py:66
  107.7 10.9 %all_to_all.138 = bf16[16,2,1440]{2,1,0:T(2,128)(2,1)S(1)} all-to-all(bf16[16,2,1440]{2,1,0:T(2,128)(2,1)S(1)} %reshape.166), channel_id=1, replica_groups=mesh['dp'=4,'gx'=4,'gy'=16] {'gy'}, dimensions={0} | all-to-all | bytes 184320 | tf_op jit(solution)/shard_map/all_to_all | solution.py:58
  122.3 9.6 %all_to_all.139 = bf16[4,2,15360]{2,1,0:T(2,128)(2,1)S(1)} all-to-all(bf16[4,2,15360]{2,1,0:T(2,128)(2,1)S(1)} %reshape.168), channel_id=1, replica_groups=mesh['dp'=4,'gx'=4,'gy'=16] {'gx'}, dimensions={0} | all-to-all | bytes 491520 | tf_op jit(solution)/shard_map/all_to_all | solution.py:60
  139.5 6.7 %reshape.142 = f32[1,16,2,20,2048]{4,3,2,1,0:T(8,128)} reshape(f32[640,2048]{1,0:T(8,128)} %convolution_add_fusion.1) | data formatting | bytes 10485760 | tf_op jit(solution)/shard_map/reshape | solution.py:63
  146.1 11.0 %fusion.4 = bf16[1,16,2,20,2048]{4,3,2,1,0:T(8,128)(2,1)} fusion(f32[1,16,2,20,2048]{4,3,2,1,0:T(8,128)} %reshape.142, bf16[1,16,2,20,2048]{4,2,3,1,0:T(2,128)(2,1)} %param.5, bf16[16,2,20,2048]{3,1,2,0:T(2,128)(2,1)} %bitcast.208, bf16[20,20]{1,0:T(8,128)(2,1)S(1)} %copy-done), kind=kOutput, calls=%fused_computation.13 | convolution fusion | flops 81264640 | bytes 13108000 | tf_op jit(solution)/shard_map/bxyip,io->bxyop/dot_general | solution.py:70
  157.1 5.3 %reshape.144 = bf16[640,2048]{1,0:T(8,128)(2,1)} reshape(bf16[1,16,2,20,2048]{4,3,2,1,0:T(8,128)(2,1)} %fusion.4) | data formatting | bytes 5242880 | tf_op jit(solution)/shard_map/reshape | solution.py:48
  168.0 3.8 reshape.161
  175.3 8.8 %all_to_all.140 = bf16[4,2,15360]{2,1,0:T(2,128)(2,1)} all-to-all(bf16[4,2,15360]{2,1,0:T(2,128)(2,1)S(1)} %reshape.170), channel_id=1, replica_groups=mesh['dp'=4,'gx'=4,'gy'=16] {'gx'}, dimensions={0} | all-to-all | bytes 491520 | tf_op jit(solution)/shard_map/all_to_all | solution.py:51
  184.2 6.0 %reshape.171 = bf16[192,16,2,20]{3,2,1,0:T(2,128)(2,1)S(1)} reshape(bf16[4,2,15360]{2,1,0:T(2,128)(2,1)} %all_to_all.140) | data formatting | bytes 491520
  196.9 5.2 %all-to-all-start.5 = ((bf16[16,2,1440]{2,1,0:T(2,128)(2,1)}), bf16[16,2,1440]{2,1,0:T(2,128)(2,1)S(1)}, u32[]{:S(2)}, u32[]{:S(2)}) async-start(bf16[16,2,1440]{2,1,0:T(2,128)(2,1)} %reshape.172), calls=%async_computation.5 | async-start | bytes 196608 | tf_op jit(solution)/shard_map/all_to_all | solution.py:53
  204.3 6.3 %all-to-all-done.5 = bf16[16,2,1440]{2,1,0:T(2,128)(2,1)S(1)} async-done(((bf16[16,2,1440]{2,1,0:T(2,128)(2,1)}), bf16[16,2,1440]{2,1,0:T(2,128)(2,1)S(1)}, u32[]{:S(2)}, u32[]{:S(2)}) %all-to-all-start.5) | async-done | bytes 92192 | tf_op jit(solution)/shard_map/all_to_all | solution.py:53
  214.5 5.0 %multiply_reduce_fusion = bf16[24,24,3,20]{1,0,2,3:T(8,128)(2,1)S(1)} fusion(f32[24,24,3,20]{1,0,2,3:T(8,128)S(1)} %copy.224, bf16[24,24,20,20,3]{1,0,4,3,2:T(8,128)(2,1)} %param.6), kind=kLoop, calls=%fused_computation.2 | loop fusion | flops 2039040 | bytes 1589760 | tf_op jit(solution)/shard_map/kloq,klcoq->klcq/dot_general | solution.py:82
  221.6 3.7 all-to-all-start.6
  225.3 4.9 fusion.31
  230.2 76.2 %psum.15 = f32[20,20]{0,1:T(8,128)S(1)} all-reduce(f32[20,20]{0,1:T(8,128)S(1)} %fusion.31), channel_id=1, replica_groups=mesh['dp'=4,'gx'=4,'gy'=16] {'dp','gx','gy'}, use_global_device_ids=true, to_apply=%region_1.2 | all-reduce | flops 400 | bytes 3200 | tf_op jit(solution)/shard_map/psum | solution.py:76
  321.4 5.3 %fusion.1 = bf16[24,24,20,20,3]{1,0,4,3,2:T(8,128)(2,1)} fusion(f32[24,24,3,20]{1,0,2,3:T(8,128)S(1)} %copy-done.3, f32[24,24,3,20]{1,0,2,3:T(8,128)} %copy.186), kind=kLoop, calls=%fused_computation.10 | loop fusion | flops 1382400 | bytes 1658880 | tf_op jit(solution)/shard_map/convert_element_type | solution.py:81
  334.4 7.2 %reshape.147 = f32[1,16,2,20,2048]{4,3,2,1,0:T(8,128)} reshape(f32[640,2048]{1,0:T(8,128)} %convolution_add_fusion) | data formatting | bytes 10485760 | tf_op jit(solution)/shard_map/reshape | solution.py:63
  341.6 4.1 fusion.12
  345.7 4.2 copy.189
  349.9 126.0 %all-reduce.2.cloned.1.call-done = bf16[24,24,20,20,3]{1,0,4,3,2:T(8,128)(2,1)} async-done(((bf16[24,24,20,20,3]{1,0,4,3,2:T(8,128)(2,1)}), bf16[24,24,20,20,3]{1,0,4,3,2:T(8,128)(2,1)}) %all-reduce.2.cloned.1.call-update) | async-done | bytes 1382416 | tf_op jit(solution)/shard_map/psum | solution.py:81
  475.9 10.2 %convert_element_type.284 = f32[24,24,20,20,3]{1,0,4,3,2:T(8,128)} convert(bf16[24,24,20,20,3]{1,0,4,3,2:T(8,128)(2,1)} %all-reduce.2.cloned.1.call-done) | non-fusion elementwise | flops 691200 | bytes 4147200 | tf_op jit(solution)/shard_map/convert_element_type | solution.py:81
  (90 shorter events, 74.8 us)
Async XLA Ops:
  7.2 139.0 %copy-start = (bf16[20,20]{1,0:T(8,128)(2,1)S(1)}, bf16[20,20]{1,0:T(8,128)(2,1)}, u32[]{:S(2)}) copy-start(bf16[20,20]{1,0:T(8,128)(2,1)} %param.7) | copy-start | bytes 2404
  60.0 10.3 %all-to-all-start = ((bf16[4,2,15360]{2,1,0:T(2,128)(2,1)}), bf16[4,2,15360]{2,1,0:T(2,128)(2,1)S(1)}, u32[]{:S(2)}, u32[]{:S(2)}) async-start(bf16[4,2,15360]{2,1,0:T(2,128)(2,1)} %reshape.162), calls=%async_computation | async-start | bytes 491520 | tf_op jit(solution)/shard_map/all_to_all | solution.py:51
  79.3 19.3 %all-to-all-start.1 = ((bf16[16,2,1440]{2,1,0:T(2,128)(2,1)}), bf16[16,2,1440]{2,1,0:T(2,128)(2,1)S(1)}, u32[]{:S(2)}, u32[]{:S(2)}) async-start(bf16[16,2,1440]{2,1,0:T(2,128)(2,1)} %reshape.164), calls=%async_computation.1 | async-start | bytes 196608 | tf_op jit(solution)/shard_map/all_to_all | solution.py:53
  119.1 16.2 %copy-start.1 = (bf16[2048,192]{0,1:T(8,128)(2,1)S(1)}, bf16[2048,192]{0,1:T(8,128)(2,1)}, u32[]{:S(2)}) copy-start(bf16[2048,192]{0,1:T(8,128)(2,1)} %convert_element_type.253) | copy-start | bytes 2359300
  196.9 13.7 %all-to-all-start.5 = ((bf16[16,2,1440]{2,1,0:T(2,128)(2,1)}), bf16[16,2,1440]{2,1,0:T(2,128)(2,1)S(1)}, u32[]{:S(2)}, u32[]{:S(2)}) async-start(bf16[16,2,1440]{2,1,0:T(2,128)(2,1)} %reshape.172), calls=%async_computation.5 | async-start | bytes 196608 | tf_op jit(solution)/shard_map/all_to_all | solution.py:53
  221.6 87.7 %all-to-all-start.6 = ((bf16[16,2,1440]{2,1,0:T(2,128)(2,1)}), bf16[16,2,1440]{2,1,0:T(2,128)(2,1)S(1)}, u32[]{:S(2)}, u32[]{:S(2)}) async-start(bf16[16,2,1440]{2,1,0:T(2,128)(2,1)} %reshape.174), calls=%async_computation.6 | async-start | bytes 196608 | tf_op jit(solution)/shard_map/all_to_all | solution.py:58
  230.2 91.2 %copy-start.3 = (f32[24,24,3,20]{1,0,2,3:T(8,128)S(1)}, f32[24,24,3,20]{1,0,2,3:T(8,128)}, u32[]{:S(2)}) copy-start(f32[24,24,3,20]{1,0,2,3:T(8,128)} %copy.187) | copy-start | bytes 414724
  317.9 9.0 %all-to-all-start.7 = ((bf16[4,2,15360]{2,1,0:T(2,128)(2,1)}), bf16[4,2,15360]{2,1,0:T(2,128)(2,1)S(1)}, u32[]{:S(2)}, u32[]{:S(2)}) async-start(bf16[4,2,15360]{2,1,0:T(2,128)(2,1)} %reshape.176), calls=%async_computation.7 | async-start | bytes 491520 | tf_op jit(solution)/shard_map/all_to_all | solution.py:60
  321.3 154.6 %all-reduce.2.cloned.1.call-start = ((), (), s32[]{:S(2)}) async-start(), calls=%async_computation.8 | async-start | bytes 14745600 | tf_op jit(solution)/shard_map/psum | solution.py:81
  334.4 7.2 %copy-start.2 = (bf16[1,16,2,20,2048]{4,3,2,1,0:T(8,128)(2,1)S(1)}, bf16[1,16,2,20,2048]{4,3,2,1,0:T(8,128)(2,1)}, u32[]{:S(2)}) copy-start(bf16[1,16,2,20,2048]{4,3,2,1,0:T(8,128)(2,1)} %fusion.4) | copy-start | bytes 7864324
Sparse Core Ops, SparseCore 0:
  326.8 149.0 all-reduce.1
where the time goes:
time: 503 us; the launch traced here: 493 us
  waiting for transfers between devices  146 us (29%)
  local copies, waits for them, and re-layouts  120 us (24%)
  blocking collectives  105 us (21%)
  matrix products  46.5 us (9%)
  other arithmetic  32.3 us (6%)
  starting transfers between devices  28 us (6%)
  between operations  15.1 us (3%)
    psum x1, waiting for transfers between devices, body(): lax.psum(local_grad.astype(jnp.bfloat16), 'dp').astype(jnp.float32)  126 us
    psum x1, blocking collectives, body(): grad_bypass = lax.psum(bypass_term, ('dp', 'gx', 'gy'))  76.2 us
    unnamed x29, local copies, waits for them, and re-layouts  39.6 us
    dot_general x12, matrix products, mode_dot(): jnp.einsum(form, data, lower, preferred_element_type=jnp.float32)  16.9 us
    all_to_all x2, starting transfers between devices, analyze(): lax.all_to_all(partial_x, 'gy', split_axis=3, concat_axis=1, tiled=True)  16.1 us
    all_to_all x2, waiting for transfers between devices, analyze(): lax.all_to_all(partial_x, 'gy', split_axis=3, concat_axis=1, tiled=True)  14.5 us
    reshape x2, local copies, waits for them, and re-layouts, synthesize(): return values.reshape(1, cells_x, cells_y, channels, NZ * NT)  13.9 us
    convert_element_type x1, local copies, waits for them, and re-layouts, mode_dot(): upper = table.astype(jnp.bfloat16)  12.3 us
  transfers between devices with their start and end apart: 6, of which 5 were waited for; matrix products, arithmetic and copies ran while one was open for 8% of the time, Pallas kernels for 0%

commit v1 on v0

--- a/solution.py
+++ b/solution.py
@@ -10,6 +10,10 @@
 MT = 4
 NZ = 128
 NT = 16
+
+
+def match_samples_all(arr_in, lane_axis="dp"):
+    return jax.lax.all_gather(arr_in, lane_axis).sum(axis=0)
 
 
 def basis(length, kept):
@@ -78,7 +82,7 @@
     local_grad = jnp.einsum(
         "klcq,kloq->klcoq", spectrum, spectrum_up, preferred_element_type=jnp.float32
     )
-    grad_spectral = lax.psum(local_grad.astype(jnp.bfloat16), "dp").astype(jnp.float32)
+    grad_spectral = match_samples_all(local_grad.astype(jnp.bfloat16)).astype(jnp.float32)
     spectrum_back = jnp.einsum(
         "kloq,klcoq->klcq", spectrum_up, spectral_weight, preferred_element_type=jnp.float32
     ).astype(jnp.bfloat16)

time: 503 us -> 520 us (1.034)
  other arithmetic: 32.3 us -> 47.7 us
  blocking collectives: 105 us -> 118 us
    psum x1 -> x0, waiting for transfers between devices: 126 us -> none  [body(): lax.psum(local_grad.astype(jnp.bfloat16), 'dp').astype(jnp.float32)]
    all_gather x0 -> x1, waiting for transfers between devices: none -> 126 us  [match_samples_all(): return jax.lax.all_gather(arr_in, lane_axis).sum(axis=0)]
    reduce_sum x0 -> x1, other arithmetic: none -> 15.3 us  [match_samples_all(): return jax.lax.all_gather(arr_in, lane_axis).sum(axis=0)]
    all_to_all x1 -> x2, blocking collectives: 10.9 us -> 21.6 us  [synthesize(): lax.all_to_all(partial_y, 'gy', split_axis=1, concat_axis=3, tiled=True)]
  transfers between devices with their start and end apart: 6 -> 5, of which waited for: 5 -> 4; matrix products, arithmetic and copies ran while one was open for 8% -> 8% of each run, Pallas kernels for 0% -> 0%
where the time goes in v1:
time: 520 us; the launch traced here: 511 us
  waiting for transfers between devices  146 us (28%)
  blocking collectives  118 us (23%)
  local copies, waits for them, and re-layouts  116 us (22%)
  other arithmetic  47.7 us (9%)
  matrix products  44.2 us (8%)
  starting transfers between devices  24.4 us (5%)
  between operations  14.7 us (3%)
    all_gather x1, waiting for transfers between devices, match_samples_all(): return jax.lax.all_gather(arr_in, lane_axis).sum(axis=0)  126 us
    psum x1, blocking collectives, body(): grad_bypass = lax.psum(bypass_term, ('dp', 'gx', 'gy'))  78.4 us
    unnamed x29, local copies, waits for them, and re-layouts  37.9 us
    all_to_all x2, blocking collectives, synthesize(): lax.all_to_all(partial_y, 'gy', split_axis=1, concat_axis=3, tiled=True)  21.6 us
    all_to_all x2, starting transfers between devices, analyze(): lax.all_to_all(partial_x, 'gy', split_axis=3, concat_axis=1, tiled=True)  16.1 us
    reduce_sum x1, other arithmetic, match_samples_all(): return jax.lax.all_gather(arr_in, lane_axis).sum(axis=0)  15.3 us
    dot_general x12, matrix products, mode_dot(): jnp.einsum(form, data, lower, preferred_element_type=jnp.float32)  15.2 us
    all_to_all x2, waiting for transfers between devices, analyze(): lax.all_to_all(partial_x, 'gy', split_axis=3, concat_axis=1, tiled=True)  14.5 us
  transfers between devices with their start and end apart: 5, of which 4 were waited for; matrix products, arithmetic and copies ran while one was open for 8% of the time, Pallas kernels for 0%

profile of v1, /device:TPU:1, one launch (start us, length us, event | category | flops | bytes accessed | tf_op | source)
XLA Modules:
  0.0 510.9 jit_solution(8396642702293125426)
XLA Ops:
  7.5 4.7 copy.145
  15.8 6.2 %fusion = (bf16[128,16,24,8]{1,0,3,2:T(8,128)(2,1)}, bf16[128,16,24,8]{1,0,3,2:T(8,128)(2,1)}) fusion(f32[16,8]{0,1:T(8,128)S(1)} %maximum_multiply_fusion.3, f32[128,24]{0,1:T(8,128)S(1)} %maximum_multiply_fusion.2), kind=kLoop, calls=%fused_computation.5 | loop fusion | flops 1966080 | bytes 1585664 | tf_op jit(solution)/shard_map/convert_element_type | solution.py:33
  22.0 11.6 %convert_element_type.258 = bf16[2048,192]{0,1:T(8,128)(2,1)S(1)} reshape(bf16[128,16,24,8]{1,0,3,2:T(8,128)(2,1)} %get-tuple-element.26) | data formatting | bytes 1572864 | tf_op jit(solution)/shard_map/convert_element_type | solution.py:33
  33.7 12.3 %convert_element_type.255 = bf16[2048,192]{0,1:T(8,128)(2,1)} reshape(bf16[128,16,24,8]{1,0,3,2:T(8,128)(2,1)} %get-tuple-element.27) | data formatting | bytes 1572864 | tf_op jit(solution)/shard_map/convert_element_type | solution.py:32
  49.9 6.0 %reshape.161 = bf16[16,2,20,192]{2,1,0,3:T(2,128)(2,1)S(1)} reshape(bf16[640,192]{0,1:T(8,128)(2,1)} %fusion.30) | data formatting | bytes 491520 | tf_op jit(solution)/shard_map/reshape | solution.py:54
  55.9 4.2 reshape.163
  60.1 4.8 all-to-all-start
  65.1 5.3 %all-to-all-done = bf16[4,2,15360]{2,1,0:T(2,128)(2,1)S(1)} async-done(((bf16[4,2,15360]{2,1,0:T(2,128)(2,1)}), bf16[4,2,15360]{2,1,0:T(2,128)(2,1)S(1)}, u32[]{:S(2)}, u32[]{:S(2)}) %all-to-all-start) | async-done | bytes 245792 | tf_op jit(solution)/shard_map/all_to_all | solution.py:55
  70.4 4.1 reshape.164
  79.3 11.0 %all-to-all-start.1 = ((bf16[16,2,1440]{2,1,0:T(2,128)(2,1)}), bf16[16,2,1440]{2,1,0:T(2,128)(2,1)S(1)}, u32[]{:S(2)}, u32[]{:S(2)}) async-start(bf16[16,2,1440]{2,1,0:T(2,128)(2,1)} %reshape.165), calls=%async_computation.1 | async-start | bytes 196608 | tf_op jit(solution)/shard_map/all_to_all | solution.py:57
  90.5 8.2 %all-to-all-done.1 = bf16[16,2,1440]{2,1,0:T(2,128)(2,1)S(1)} async-done(((bf16[16,2,1440]{2,1,0:T(2,128)(2,1)}), bf16[16,2,1440]{2,1,0:T(2,128)(2,1)S(1)}, u32[]{:S(2)}, u32[]{:S(2)}) %all-to-all-start.1) | async-done | bytes 92192 | tf_op jit(solution)/shard_map/all_to_all | solution.py:57
  101.2 5.0 multiply_reduce_fusion.1
  107.7 10.9 %all_to_all.138 = bf16[16,2,1440]{2,1,0:T(2,128)(2,1)S(1)} all-to-all(bf16[16,2,1440]{2,1,0:T(2,128)(2,1)S(1)} %reshape.167), channel_id=1, replica_groups=mesh['dp'=4,'gx'=4,'gy'=16] {'gy'}, dimensions={0} | all-to-all | bytes 184320 | tf_op jit(solution)/shard_map/all_to_all | solution.py:62
  122.4 9.6 %all_to_all.139 = bf16[4,2,15360]{2,1,0:T(2,128)(2,1)S(1)} all-to-all(bf16[4,2,15360]{2,1,0:T(2,128)(2,1)S(1)} %reshape.169), channel_id=1, replica_groups=mesh['dp'=4,'gx'=4,'gy'=16] {'gx'}, dimensions={0} | all-to-all | bytes 491520 | tf_op jit(solution)/shard_map/all_to_all | solution.py:64
  139.6 6.7 %reshape.142 = f32[1,16,2,20,2048]{4,3,2,1,0:T(8,128)} reshape(f32[640,2048]{1,0:T(8,128)} %convolution_add_fusion.1) | data formatting | bytes 10485760 | tf_op jit(solution)/shard_map/reshape | solution.py:67
  146.3 11.0 %fusion.4 = bf16[1,16,2,20,2048]{4,3,2,1,0:T(8,128)(2,1)} fusion(f32[1,16,2,20,2048]{4,3,2,1,0:T(8,128)} %reshape.142, bf16[1,16,2,20,2048]{4,2,3,1,0:T(2,128)(2,1)} %param.5, bf16[16,2,20,2048]{3,1,2,0:T(2,128)(2,1)} %bitcast.210, bf16[20,20]{1,0:T(8,128)(2,1)S(1)} %copy-done), kind=kOutput, calls=%fused_computation.13 | convolution fusion | flops 81264640 | bytes 13108000 | tf_op jit(solution)/shard_map/bxyip,io->bxyop/dot_general | solution.py:74
  157.3 5.3 %reshape.144 = bf16[640,2048]{1,0:T(8,128)(2,1)} reshape(bf16[1,16,2,20,2048]{4,3,2,1,0:T(8,128)(2,1)} %fusion.4) | data formatting | bytes 5242880 | tf_op jit(solution)/shard_map/reshape | solution.py:52
  175.5 8.8 %all_to_all.140 = bf16[4,2,15360]{2,1,0:T(2,128)(2,1)} all-to-all(bf16[4,2,15360]{2,1,0:T(2,128)(2,1)S(1)} %reshape.171), channel_id=1, replica_groups=mesh['dp'=4,'gx'=4,'gy'=16] {'gx'}, dimensions={0} | all-to-all | bytes 491520 | tf_op jit(solution)/shard_map/all_to_all | solution.py:55
  184.3 6.0 %reshape.172 = bf16[192,16,2,20]{3,2,1,0:T(2,128)(2,1)S(1)} reshape(bf16[4,2,15360]{2,1,0:T(2,128)(2,1)} %all_to_all.140) | data formatting | bytes 491520
  197.1 5.2 %all-to-all-start.5 = ((bf16[16,2,1440]{2,1,0:T(2,128)(2,1)}), bf16[16,2,1440]{2,1,0:T(2,128)(2,1)S(1)}, u32[]{:S(2)}, u32[]{:S(2)}) async-start(bf16[16,2,1440]{2,1,0:T(2,128)(2,1)} %reshape.173), calls=%async_computation.5 | async-start | bytes 196608 | tf_op jit(solution)/shard_map/all_to_all | solution.py:57
  204.5 6.2 %all-to-all-done.5 = bf16[16,2,1440]{2,1,0:T(2,128)(2,1)S(1)} async-done(((bf16[16,2,1440]{2,1,0:T(2,128)(2,1)}), bf16[16,2,1440]{2,1,0:T(2,128)(2,1)S(1)}, u32[]{:S(2)}, u32[]{:S(2)}) %all-to-all-start.5) | async-done | bytes 92192 | tf_op jit(solution)/shard_map/all_to_all | solution.py:57
  214.7 5.4 %fusion.1 = bf16[24,24,20,20,3]{1,0,4,3,2:T(8,128)(2,1)} fusion(f32[24,24,3,20]{1,0,2,3:T(8,128)} %copy.187, f32[24,24,3,20]{1,0,2,3:T(8,128)S(1)} %copy.186), kind=kLoop, calls=%fused_computation.10 | loop fusion | flops 1382400 | bytes 1658880 | tf_op jit(solution)/shard_map/convert_element_type | solution.py:85
  220.4 5.0 multiply_reduce_fusion
  226.9 10.8 %all_to_all.141 = bf16[16,2,1440]{2,1,0:T(2,128)(2,1)S(1)} all-to-all(bf16[16,2,1440]{2,1,0:T(2,128)(2,1)S(1)} %reshape.175), channel_id=1, replica_groups=mesh['dp'=4,'gx'=4,'gy'=16] {'gy'}, dimensions={0} | all-to-all | bytes 184320 | tf_op jit(solution)/shard_map/all_to_all | solution.py:62
  245.5 5.1 %fusion.31 = f32[20,20]{0,1:T(8,128)S(1)} fusion(bf16[16,2,20,2048]{3,1,2,0:T(2,128)(2,1)} %bitcast.211, bf16[1,16,2,20,2048]{4,3,2,1,0:T(8,128)(2,1)} %fusion.4), kind=kOutput, calls=%fused_computation.54 | convolution fusion | flops 52428800 | bytes 5244480 | tf_op jit(solution)/shard_map/bxyip,bxyop->io/dot_general | solution.py:79
  250.6 78.4 %psum.7 = f32[20,20]{0,1:T(8,128)S(1)} all-reduce(f32[20,20]{0,1:T(8,128)S(1)} %fusion.31), channel_id=1, replica_groups=mesh['dp'=4,'gx'=4,'gy'=16] {'dp','gx','gy'}, use_global_device_ids=true, to_apply=%region_1.2 | all-reduce | flops 400 | bytes 3200 | tf_op jit(solution)/shard_map/psum | solution.py:80
  337.2 7.0 %reshape.147 = f32[1,16,2,20,2048]{4,3,2,1,0:T(8,128)} reshape(f32[640,2048]{1,0:T(8,128)} %convolution_add_fusion) | data formatting | bytes 10485760 | tf_op jit(solution)/shard_map/reshape | solution.py:67
  344.2 4.1 fusion.12
  348.3 4.2 copy.189
  352.6 125.8 %all-gather.3.cloned.1.call-done = bf16[96,24,20,20,3]{1,0,4,3,2:T(8,128)(2,1)} async-done(((bf16[24,24,20,20,3]{1,0,4,3,2:T(8,128)(2,1)}), bf16[96,24,20,20,3]{1,0,4,3,2:T(8,128)(2,1)}) %all-gather.3.cloned.1.call-update) | async-done | bytes 5529616 | tf_op jit(solution)/shard_map/all_gather | solution.py:16
  478.3 15.3 %reduce_sum.12 = bf16[24,24,20,20,3]{1,0,4,3,2:T(8,128)(2,1)} reduce(bf16[4,24,24,20,20,3]{2,1,0,5,4,3:T(8,128)(2,1)} %bitcast.197, bf16[]{:T(256)} %constant.110.clone.1), dimensions={0}, to_apply=%region_0.1 | reduce | flops 2073600 | bytes 6912002 | tf_op jit(solution)/shard_map/reduce_sum | solution.py:16
  493.7 10.2 %convert_element_type.286 = f32[24,24,20,20,3]{1,0,4,3,2:T(8,128)} convert(bf16[24,24,20,20,3]{1,0,4,3,2:T(8,128)(2,1)} %reduce_sum.12) | non-fusion elementwise | flops 691200 | bytes 4147200 | tf_op jit(solution)/shard_map/convert_element_type | solution.py:85
  (90 shorter events, 71.6 us)
Async XLA Ops:
  7.2 139.1 %copy-start = (bf16[20,20]{1,0:T(8,128)(2,1)S(1)}, bf16[20,20]{1,0:T(8,128)(2,1)}, u32[]{:S(2)}) copy-start(bf16[20,20]{1,0:T(8,128)(2,1)} %param.7) | copy-start | bytes 2404
  60.1 10.3 %all-to-all-start = ((bf16[4,2,15360]{2,1,0:T(2,128)(2,1)}), bf16[4,2,15360]{2,1,0:T(2,128)(2,1)S(1)}, u32[]{:S(2)}, u32[]{:S(2)}) async-start(bf16[4,2,15360]{2,1,0:T(2,128)(2,1)} %reshape.163), calls=%async_computation | async-start | bytes 491520 | tf_op jit(solution)/shard_map/all_to_all | solution.py:55
  79.3 19.3 %all-to-all-start.1 = ((bf16[16,2,1440]{2,1,0:T(2,128)(2,1)}), bf16[16,2,1440]{2,1,0:T(2,128)(2,1)S(1)}, u32[]{:S(2)}, u32[]{:S(2)}) async-start(bf16[16,2,1440]{2,1,0:T(2,128)(2,1)} %reshape.165), calls=%async_computation.1 | async-start | bytes 196608 | tf_op jit(solution)/shard_map/all_to_all | solution.py:57
  119.2 16.3 %copy-start.1 = (bf16[2048,192]{0,1:T(8,128)(2,1)S(1)}, bf16[2048,192]{0,1:T(8,128)(2,1)}, u32[]{:S(2)}) copy-start(bf16[2048,192]{0,1:T(8,128)(2,1)} %convert_element_type.255) | copy-start | bytes 2359300
  197.1 13.7 %all-to-all-start.5 = ((bf16[16,2,1440]{2,1,0:T(2,128)(2,1)}), bf16[16,2,1440]{2,1,0:T(2,128)(2,1)S(1)}, u32[]{:S(2)}, u32[]{:S(2)}) async-start(bf16[16,2,1440]{2,1,0:T(2,128)(2,1)} %reshape.173), calls=%async_computation.5 | async-start | bytes 196608 | tf_op jit(solution)/shard_map/all_to_all | solution.py:57
  202.2 276.1 %all-gather.3.cloned.1.call-start = ((), (), s32[]{:S(2)}) async-start(), calls=%async_computation.8 | async-start | bytes 36864000 | tf_op jit(solution)/shard_map/all_gather | solution.py:16
  214.7 5.4 %copy-start.3 = (f32[24,24,3,20]{0,1,2,3:T(8,128)S(1)}, f32[24,24,3,20]{0,1,2,3:T(8,128)}, u32[]{:S(2)}) copy-start(f32[24,24,3,20]{0,1,2,3:T(8,128)} %get-tuple-element.19) | copy-start | bytes 414724
  242.1 87.6 %all-to-all-start.7 = ((bf16[4,2,15360]{2,1,0:T(2,128)(2,1)}), bf16[4,2,15360]{2,1,0:T(2,128)(2,1)S(1)}, u32[]{:S(2)}, u32[]{:S(2)}) async-start(bf16[4,2,15360]{2,1,0:T(2,128)(2,1)} %reshape.177), calls=%async_computation.7 | async-start | bytes 491520 | tf_op jit(solution)/shard_map/all_to_all | solution.py:64
  337.2 7.0 %copy-start.2 = (bf16[1,16,2,20,2048]{4,3,2,1,0:T(8,128)(2,1)S(1)}, bf16[1,16,2,20,2048]{4,3,2,1,0:T(8,128)(2,1)}, u32[]{:S(2)}) copy-start(bf16[1,16,2,20,2048]{4,3,2,1,0:T(8,128)(2,1)} %fusion.4) | copy-start | bytes 7864324
Sparse Core Ops, SparseCore 0:
  220.3 258.0 all-gather.2
